TPU v7x, 32 devices: a whole 2x2x4 slice. The times are simulated.
32 devices in a mesh: groups: 2 (over x), wide: 8 (over z, y), narrow: 2 (over core).
Axes of the slice: x: 2, y: 2, z: 4, core: 2. Of those that a mesh axis runs over, the one named last changes fastest.
Arguments:
- splats: float32 [16, 262144], P(None, ('groups', 'wide')), parts along dimension 1, may hold values from -16 to 1024, as said below
- send_slots: int32 [16, 2, 8192], P(('groups', 'wide'), 'narrow'), parts along dimension 0, may hold values from 0 to 16383, as said below
- tile_lists: int32 [16, 64, 256], P(('groups', 'wide'), 'narrow'), parts along dimension 0, may hold values from 0 to 8191, as said below
- tile_lengths: int32 [16, 64], P(('groups', 'wide'), 'narrow'), parts along dimension 0, may hold values from 32 to 256, as said below
- pixel_grads: float32 [10, 16, 64, 256], P(None, ('groups', 'wide'), 'narrow'), parts along dimension 1, may hold values from -6 to 6
Outputs:
- splat_grads: float32 [16, 262144], P(None, ('groups', 'wide')), parts along dimension 1
There are 2 independent parts, one for each index of `groups`. A program takes and returns all parts, laid end to end along the dimension named above; each array names one. Nothing has to cross between parts.
Inputs may be any that keep to these rules, and one draw needn't show every extreme that they name: send_slots[s, n, t * 1024 + c] is the local index (within the column's 16384) of the splat in slot c of what column s sends to the device of column t and half n. A splat fills at most two slots over all devices (one for each tile it is listed in); some splats fill none. `tile_lists`: receive slot s * 1024 + c of a device is slot c of what column s sends it. The first tile_lengths entries of a tile are distinct slots, and no slot is among the live entries of two tiles of one device; entries past the length are arbitrary slots. `tile_lengths`: in every draw some tile holds exactly 256 live entries. `splats`: rows 0 and 1 are a splat's centre in pixels (tile (t, r) covers x from 16 t to 16 t + 16 and y from 16 r to 16 r + 16); rows 2, 3, 4 a conic (a, b, c) with a > 0 and a c > b b; row 5 an opacity logit of at most -1; rows 6 onward its channels.
All inputs are finite; a program needn't handle non-finite values.
Results may differ from a plain program's by a relative error of at most 0.0003.
Values sent between devices are 32-bit elements; how exact they have to be, the bound alone decides.
A program may use at most 64 MiB of HBM per device.

v0:
```python
import math

import jax
import jax.numpy as jnp
from jax import lax
from jax.sharding import PartitionSpec as P


def tile_image(params, lengths, starts_x, starts_y):
    list_depth = params.shape[2]
    pixel_index = jnp.arange(256)
    pixel_x = (pixel_index % 16).astype(jnp.float32) + 0.5
    pixel_y = (pixel_index // 16).astype(jnp.float32) + 0.5
    pos_x = (starts_x[:, None] + pixel_x[None, :])[:, None, :]
    pos_y = (starts_y[:, None] + pixel_y[None, :])[:, None, :]
    delta_x = pos_x - params[0][:, :, None]
    delta_y = pos_y - params[1][:, :, None]
    exponent = (
        -0.5
        * (params[2][:, :, None] * delta_x * delta_x + params[4][:, :, None] * delta_y * delta_y)
        - params[3][:, :, None] * delta_x * delta_y
    )
    active_mask = (jnp.arange(list_depth)[None, :] < lengths[:, None]).astype(jnp.float32)
    opacity = jax.nn.sigmoid(params[5]) * active_mask
    alpha_value = opacity[:, :, None] * jnp.exp(exponent)
    log_clear = jnp.log1p(-alpha_value)
    before = jnp.cumsum(log_clear, axis=1) - log_clear
    weight = jnp.exp(before) * alpha_value
    return jnp.einsum("bkp,cbk->cbp", weight, params[6:], precision=lax.Precision.HIGHEST)


def body(splats, send_slots, tile_lists, tile_lengths, pixel_grads):
    features = splats.shape[0]
    local_count = splats.shape[1]
    slot_count = send_slots.shape[2]
    tile_count = tile_lists.shape[1]
    list_depth = tile_lists.shape[2]
    entry_count = tile_count * list_depth
    sent_index = send_slots.reshape(slot_count)
    outgoing = jnp.take(splats, sent_index, axis=1)
    received = lax.all_to_all(outgoing, "wide", split_axis=1, concat_axis=1, tiled=True)
    tile_block = math.gcd(tile_count, 8)
    column_x = (lax.axis_index("wide") * 16).astype(jnp.float32)
    row_base = lax.axis_index("narrow") * tile_count
    lists_here = tile_lists[0]
    lengths_here = tile_lengths[0]
    grads_here = pixel_grads[:, 0]
    all_params = jnp.take(received, lists_here.reshape(entry_count), axis=1).reshape(
        features, tile_count, list_depth
    )

    def block_step(step_index, stacked):
        first_tile = step_index * tile_block
        params = lax.dynamic_slice_in_dim(all_params, first_tile, tile_block, 1)
        lengths_block = lax.dynamic_slice_in_dim(lengths_here, first_tile, tile_block, 0)
        cotangent = lax.dynamic_slice_in_dim(grads_here, first_tile, tile_block, 1)
        row_start = ((row_base + first_tile + jnp.arange(tile_block)) * 16).astype(jnp.float32)
        starts_x = jnp.zeros((tile_block,), jnp.float32) + column_x
        rendered, pullback = jax.vjp(
            lambda values: tile_image(values, lengths_block, starts_x, row_start), params
        )
        entry_grads = pullback(cotangent)[0]
        return lax.dynamic_update_slice_in_dim(stacked, entry_grads, first_tile, 1)

    stacked = lax.fori_loop(
        0,
        tile_count // tile_block,
        block_step,
        jnp.zeros((features, tile_count, list_depth), jnp.float32),
    )
    live_entry = jnp.arange(list_depth)[None, :] < lengths_here[:, None]
    live_target = jnp.where(live_entry, lists_here, slot_count).reshape(entry_count)
    entry_number = jnp.arange(entry_count)
    slot_source = (
        jnp.full((slot_count,), entry_count, jnp.int32)
        .at[live_target]
        .set(entry_number, mode="drop")
    )
    padded_grads = jnp.concatenate(
        [stacked.reshape(features, entry_count), jnp.zeros((features, 1), jnp.float32)], axis=1
    )
    slot_grads = jnp.take(padded_grads, slot_source, axis=1)
    returned = lax.all_to_all(slot_grads, "wide", split_axis=1, concat_axis=1, tiled=True)
    partial_grads = jnp.zeros((features, local_count), jnp.float32).at[:, sent_index].add(returned)
    return lax.psum(partial_grads, "narrow")


def solution(mesh):
    placed = (
        P(None, ("groups", "wide")),
        P(("groups", "wide"), "narrow", None),
        P(("groups", "wide"), "narrow", None),
        P(("groups", "wide"), "narrow"),
        P(None, ("groups", "wide"), "narrow", None),
    )
    return jax.shard_map(
        body, mesh=mesh, in_specs=placed, out_specs=P(None, ("groups", "wide")), check_vma=False
    )
```

profile of v0, /device:TPU:0, one launch (start us, length us, event | category | flops | bytes accessed | tf_op | source)
XLA Modules:
  0.0 419.0 jit_solution(8209377224956155588)
XLA Ops:
  9.4 6.0 %copy.59 = f32[16,16384]{0,1:T(8,128)} copy(f32[16,16384]{1,0:T(8,128)} %param.7) | data formatting | bytes 2097152 | tf_op args[0]
  15.3 31.1 %gather_fusion = f32[8192,16]{1,0:T(8,128)} fusion(f32[16,16384]{0,1:T(8,128)} %copy.59, s32[8192]{0:T(1024)S(1)} %broadcast_clamp_fusion.1), kind=kCustom, calls=%fused_computation | custom fusion | bytes 1081344 | tf_op jit(solution)/shard_map/jit(_take)/gather | solution.py:40
  50.1 7.3 %all-to-all-start = ((f32[16,8,1024]{2,0,1:T(8,128)}), f32[16,8,1024]{2,0,1:T(8,128)S(1)}, u32[]{:S(2)}, u32[]{:S(2)}) async-start(f32[16,8,1024]{2,0,1:T(8,128)} %broadcast_select_fusion.2), calls=%async_computation | async-start | bytes 1048576 | tf_op jit(solution)/shard_map/all_to_all | solution.py:41
  57.7 30.5 %scatter_custom_fusion = s32[8192]{0:T(1024)S(1)} fusion(s32[8192]{0:T(1024)S(1)} %bitcast.164, s32[8192]{0:T(1024)S(1)} %iota.72, s32[]{:T(128)} %constant.203.clone.1), kind=kCustom, calls=%fused_computation.156 | custom fusion | bytes 32772 | tf_op jit(solution)/shard_map/scatter | solution.py:77
  91.9 29.9 %gather_fusion.1 = f32[8192,16]{1,0:T(8,128)} fusion(f32[16,8192]{0,1:T(8,128)} %bitcast.141, s32[8192]{0:T(1024)S(1)} %broadcast_clamp_fusion), kind=kCustom, calls=%fused_computation.1 | custom fusion | bytes 1081344 | tf_op jit(solution)/shard_map/jit(_take)/gather | solution.py:48
  124.8 133.6 %while.15 = (s32[]{:T(128)}, f32[16,32,256]{2,0,1:T(8,128)S(1)}, f32[10,32,256]{2,0,1:T(8,128)}, s32[32]{0:T(128)S(1)}, f32[16,32,256]{2,0,1:T(8,128)S(1)}, /*in...) while((s32[]{:T(128)}, f32[16,32,256]{2,0,1:T(8,128)S(1)}, ...), condition=%wide.region_12.13_spmd, body=%wide.region_1.12_spmd.sunk | while | flops 309562144 | bytes 52046916 | solution.py:65
  130.2 4.7 %fusion.107 = f32[10,8,256]{2,0,1:T(8,128)S(1)} fusion(f32[8,256,256]{2,1,0:T(8,128)} %copy.126, f32[8,256]{1,0:T(8,128)S(1)} %get-tuple-element.292, f32[8,256]{1,0:T(8,128)S(1)} %get-tuple-element.286, f32[8,256]{1,0:T(8,128)S(1)} %broadcast_add_fusion.6, f32[8,256]{1,0:T(8,128)S(1)} %get-tuple-element.293, f32[8,256]{1,0:T(8,128)S(1)} %get-tuple-element.290, ...), kind=kOutput, calls=%fused_computation.75.clone.1 | convolution fusion | flops 70778880 | bytes 2368516 | tf_op jit(solution)/shard_map/while/body/eval_jaxpr/transpose(jvp(bkp,cbk->cbp))/dot_general | solution.py:29
  134.9 6.1 %fusion.102 = (f32[8,256,256]{1,2,0:T(8,128)S(1)}, f32[8,256,256]{2,1,0:T(8,128)}) fusion(f32[8,256,256]{1,0,2:T(8,128)S(1)} %bitcast.138, f32[8,256]{1,0:T(8,128)S(1)} %get-tuple-element.292, f32[8,256]{1,0:T(8,128)S(1)} %get-tuple-element.286, f32[8,256]{1,0:T(8,128)S(1)} %broadcast_add_fusion.6, f32[8,256]{1,0:T(8,128)S(1)} %get-tuple-element.293, ...), kind=kOutput, calls=%fused_computation.64.clone.1 | convolution fusion | flops 71303168 | bytes 6613504 | tf_op jit(solution)/shard_map/while/body/eval_jaxpr/transpose(jvp(bkp,cbk->cbp))/dot_general | solution.py:29
  141.0 5.0 %fusion.103 = f32[8,256,2,128]{1,0,3,2:T(8,128)S(1)} fusion(f32[8,256,2,128]{1,3,2,0:T(8,128)S(1)} %bitcast.140), kind=kOutput, calls=%fused_computation.68.clone.1 | output fusion | flops 66584576 | bytes 4194304 | tf_op jit(solution)/shard_map/reduce-window.22
  151.1 6.8 %fusion.105 = (f32[8,256]{1,0:T(8,128)S(1)}, f32[8,256]{1,0:T(8,128)S(1)}, f32[8,256]{1,0:T(8,128)S(1)}, f32[8,256]{1,0:T(8,128)S(1)}, f32[8,256]{1,0:T(8,128)S(1)}, /*index=5*/f32[8,256]{1,0:T(8,128)S(1)}) fusion(f32[8,256]{1,0:T(8,128)S(1)} %get-tuple-element.286, f32[8,256]{1,0:T(8,128)S(1)} %broadcast_add_fusion.6, ...), kind=kLoop, calls=%fused_computation.55.clone.1 | loop fusion | flops 26202112 | bytes 6398976 | tf_op jit(solution)/shard_map/while/body/eval_jaxpr/transpose(jvp())/reduce_sum | solution.py:21
  168.2 6.1 %fusion.102 = (f32[8,256,256]{1,2,0:T(8,128)S(1)}, f32[8,256,256]{2,1,0:T(8,128)}) fusion(f32[8,256,256]{1,0,2:T(8,128)S(1)} %bitcast.138, f32[8,256]{1,0:T(8,128)S(1)} %get-tuple-element.292, f32[8,256]{1,0:T(8,128)S(1)} %get-tuple-element.286, f32[8,256]{1,0:T(8,128)S(1)} %broadcast_add_fusion.6, f32[8,256]{1,0:T(8,128)S(1)} %get-tuple-element.293, ...), kind=kOutput, calls=%fused_computation.64.clone.1 | convolution fusion | flops 71303168 | bytes 6613504 | tf_op jit(solution)/shard_map/while/body/eval_jaxpr/transpose(jvp(bkp,cbk->cbp))/dot_general | solution.py:29
  174.3 5.0 %fusion.103 = f32[8,256,2,128]{1,0,3,2:T(8,128)S(1)} fusion(f32[8,256,2,128]{1,3,2,0:T(8,128)S(1)} %bitcast.140), kind=kOutput, calls=%fused_computation.68.clone.1 | output fusion | flops 66584576 | bytes 4194304 | tf_op jit(solution)/shard_map/reduce-window.22
  184.4 6.8 %fusion.105 = (f32[8,256]{1,0:T(8,128)S(1)}, f32[8,256]{1,0:T(8,128)S(1)}, f32[8,256]{1,0:T(8,128)S(1)}, f32[8,256]{1,0:T(8,128)S(1)}, f32[8,256]{1,0:T(8,128)S(1)}, /*index=5*/f32[8,256]{1,0:T(8,128)S(1)}) fusion(f32[8,256]{1,0:T(8,128)S(1)} %get-tuple-element.286, f32[8,256]{1,0:T(8,128)S(1)} %broadcast_add_fusion.6, ...), kind=kLoop, calls=%fused_computation.55.clone.1 | loop fusion | flops 26202112 | bytes 6398976 | tf_op jit(solution)/shard_map/while/body/eval_jaxpr/transpose(jvp())/reduce_sum | solution.py:21
  201.5 6.1 %fusion.102 = (f32[8,256,256]{1,2,0:T(8,128)S(1)}, f32[8,256,256]{2,1,0:T(8,128)}) fusion(f32[8,256,256]{1,0,2:T(8,128)S(1)} %bitcast.138, f32[8,256]{1,0:T(8,128)S(1)} %get-tuple-element.292, f32[8,256]{1,0:T(8,128)S(1)} %get-tuple-element.286, f32[8,256]{1,0:T(8,128)S(1)} %broadcast_add_fusion.6, f32[8,256]{1,0:T(8,128)S(1)} %get-tuple-element.293, ...), kind=kOutput, calls=%fused_computation.64.clone.1 | convolution fusion | flops 71303168 | bytes 6613504 | tf_op jit(solution)/shard_map/while/body/eval_jaxpr/transpose(jvp(bkp,cbk->cbp))/dot_general | solution.py:29
  207.6 5.0 %fusion.103 = f32[8,256,2,128]{1,0,3,2:T(8,128)S(1)} fusion(f32[8,256,2,128]{1,3,2,0:T(8,128)S(1)} %bitcast.140), kind=kOutput, calls=%fused_computation.68.clone.1 | output fusion | flops 66584576 | bytes 4194304 | tf_op jit(solution)/shard_map/reduce-window.22
  217.8 6.8 %fusion.105 = (f32[8,256]{1,0:T(8,128)S(1)}, f32[8,256]{1,0:T(8,128)S(1)}, f32[8,256]{1,0:T(8,128)S(1)}, f32[8,256]{1,0:T(8,128)S(1)}, f32[8,256]{1,0:T(8,128)S(1)}, /*index=5*/f32[8,256]{1,0:T(8,128)S(1)}) fusion(f32[8,256]{1,0:T(8,128)S(1)} %get-tuple-element.286, f32[8,256]{1,0:T(8,128)S(1)} %broadcast_add_fusion.6, ...), kind=kLoop, calls=%fused_computation.55.clone.1 | loop fusion | flops 26202112 | bytes 6398976 | tf_op jit(solution)/shard_map/while/body/eval_jaxpr/transpose(jvp())/reduce_sum | solution.py:21
  234.8 6.1 %fusion.102 = (f32[8,256,256]{1,2,0:T(8,128)S(1)}, f32[8,256,256]{2,1,0:T(8,128)}) fusion(f32[8,256,256]{1,0,2:T(8,128)S(1)} %bitcast.138, f32[8,256]{1,0:T(8,128)S(1)} %get-tuple-element.292, f32[8,256]{1,0:T(8,128)S(1)} %get-tuple-element.286, f32[8,256]{1,0:T(8,128)S(1)} %broadcast_add_fusion.6, f32[8,256]{1,0:T(8,128)S(1)} %get-tuple-element.293, ...), kind=kOutput, calls=%fused_computation.64.clone.1 | convolution fusion | flops 71303168 | bytes 6613504 | tf_op jit(solution)/shard_map/while/body/eval_jaxpr/transpose(jvp(bkp,cbk->cbp))/dot_general | solution.py:29
  240.9 5.0 %fusion.103 = f32[8,256,2,128]{1,0,3,2:T(8,128)S(1)} fusion(f32[8,256,2,128]{1,3,2,0:T(8,128)S(1)} %bitcast.140), kind=kOutput, calls=%fused_computation.68.clone.1 | output fusion | flops 66584576 | bytes 4194304 | tf_op jit(solution)/shard_map/reduce-window.22
  251.1 6.8 %fusion.105 = (f32[8,256]{1,0:T(8,128)S(1)}, f32[8,256]{1,0:T(8,128)S(1)}, f32[8,256]{1,0:T(8,128)S(1)}, f32[8,256]{1,0:T(8,128)S(1)}, f32[8,256]{1,0:T(8,128)S(1)}, /*index=5*/f32[8,256]{1,0:T(8,128)S(1)}) fusion(f32[8,256]{1,0:T(8,128)S(1)} %get-tuple-element.286, f32[8,256]{1,0:T(8,128)S(1)} %broadcast_add_fusion.6, ...), kind=kLoop, calls=%fused_computation.55.clone.1 | loop fusion | flops 26202112 | bytes 6398976 | tf_op jit(solution)/shard_map/while/body/eval_jaxpr/transpose(jvp())/reduce_sum | solution.py:21
  264.7 30.1 %gather_fusion.2 = f32[8192,16]{1,0:T(8,128)} fusion(f32[16,8193]{0,1:T(8,128)} %concatenate.3, s32[8192]{0:T(1024)S(1)} %fusion.79), kind=kCustom, calls=%fused_computation.2 | custom fusion | bytes 1081344 | tf_op jit(solution)/shard_map/jit(_take)/gather | solution.py:82
  297.7 19.7 %all_to_all.18 = f32[16,8,1024]{2,0,1:T(8,128)S(1)} all-to-all(f32[16,8,1024]{2,0,1:T(8,128)S(1)} %broadcast_select_fusion.1), channel_id=1, replica_groups=mesh['groups'=2,'wide'=8,'narrow'=2] {'wide'}, dimensions={1} | all-to-all | bytes 1048576 | tf_op jit(solution)/shard_map/all_to_all | solution.py:83
  320.1 48.0 %scatter_custom_fusion.1 = f32[16,16384]{0,1:T(8,128)} fusion(s32[8192]{0:T(1024)S(1)} %bitcast.160, f32[8192,16]{1,0:T(8,128)} %copy.66, f32[]{:T(128)} %constant.200.clone.1), kind=kCustom, calls=%fused_computation.136 | custom fusion | flops 131072 | bytes 1049088 | tf_op jit(solution)/shard_map/scatter-add | solution.py:84
  368.1 38.1 %all-reduce.10.cloned.1.call-done = f32[16,16384]{0,1:T(8,128)} async-done(((f32[16,16384]{0,1:T(8,128)}), f32[16,16384]{0,1:T(8,128)}) %all-reduce.10.cloned.1.call-update) | async-done | bytes 1048592 | tf_op jit(solution)/shard_map/psum | solution.py:85
  406.2 6.0 %copy.67 = f32[16,16384]{1,0:T(8,128)} copy(f32[16,16384]{0,1:T(8,128)} %all-reduce.10.cloned.1.call-done) | data formatting | bytes 2097152 | tf_op jit(solution)/shard_map/psum | solution.py:85
  (193 shorter events, 81.1 us)
Async XLA Ops:
  49.2 8.2 %copy-start.3 = (s32[1,32]{1,0:T(1,128)S(1)}, s32[1,32]{1,0:T(1,128)}, u32[]{:S(2)}) copy-start(s32[1,32]{1,0:T(1,128)} %param.10) | copy-start | bytes 388
  49.2 8.3 %copy-start.2 = (s32[1,32,256]{2,1,0:T(8,128)S(1)}, s32[1,32,256]{2,1,0:T(8,128)}, u32[]{:S(2)}) copy-start(s32[1,32,256]{2,1,0:T(8,128)} %param.9) | copy-start | bytes 98308
  49.2 39.0 %copy-start.1 = (f32[10,1,32,256]{3,2,1,0:T(8,128)S(1)}, f32[10,1,32,256]{3,2,1,0:T(8,128)}, u32[]{:S(2)}) copy-start(f32[10,1,32,256]{3,2,1,0:T(8,128)} %param.11) | copy-start | bytes 983044
  50.1 39.2 %all-to-all-start = ((f32[16,8,1024]{2,0,1:T(8,128)}), f32[16,8,1024]{2,0,1:T(8,128)S(1)}, u32[]{:S(2)}, u32[]{:S(2)}) async-start(f32[16,8,1024]{2,0,1:T(8,128)} %broadcast_select_fusion.2), calls=%async_computation | async-start | bytes 1048576 | tf_op jit(solution)/shard_map/all_to_all | solution.py:41
  57.4 348.8 %all-reduce.10.cloned.1.call-start = ((), (), s32[]{:S(2)}) async-start(), calls=%async_computation.2 | async-start | bytes 16777216 | tf_op jit(solution)/shard_map/psum | solution.py:85
  148.1 3.1 copy-start
  181.4 3.1 copy-start
  214.7 3.1 copy-start
  248.0 3.1 copy-start
Sparse Core Ops, SparseCore 0:
  368.2 37.9 all-reduce.9
where the time goes:
time: 420 us; the launch traced here: 419 us
  local copies, waits for them, and re-layouts  186 us (44%)
  other arithmetic  110 us (26%)
  matrix products  43.3 us (10%)
  waiting for transfers between devices  38.1 us (9%)
  blocking collectives  19.7 us (5%)
  between operations  13.6 us (3%)
  starting transfers between devices  7.32 us (2%)
    scatter-add x1, other arithmetic, body(): jnp.zeros((features, local_count), jnp.float32).at[:, sent_index]  48 us
    dot_general x8, matrix products, tile_image(): jnp.einsum('bkp,cbk->cbp', weight, params[6:], precision=lax.Precision.HI...  43.3 us
    psum x1, waiting for transfers between devices, body(): return lax.psum(partial_grads, 'narrow')  38.1 us
    gather x2, local copies, waits for them, and re-layouts, body(): outgoing = jnp.take(splats, sent_index, axis=1)  33.9 us
    gather x2, local copies, waits for them, and re-layouts, body(): slot_grads = jnp.take(padded_grads, slot_source, axis=1)  32.9 us
    gather x2, local copies, waits for them, and re-layouts, body(): jnp.take(received, lists_here.reshape(entry_count), axis=1)  32.7 us
    scatter x1, local copies, waits for them, and re-layouts, body(): slot_source = jnp.full((slot_count,), entry_count, jnp.int32).at[live_tar...  30.5 us
    another operation x24, other arithmetic  29.1 us
  transfers between devices with their start and end apart: 2, of which 1 were waited for; matrix products, arithmetic and copies ran while one was open for 8% of the time, Pallas kernels for 0%

commit v1 on v0

v1 whole, which is shorter than its diff:
```python
import functools
import math

import jax
import jax.numpy as jnp
from jax import lax
from jax.experimental import pallas as pl
from jax.experimental.pallas import tpu as pltpu
from jax.sharding import PartitionSpec as P

LANES = 128
F32 = jnp.float32
BF16 = jnp.bfloat16
LOG2E = math.log2(math.e)
VMEM_BYTES = 48 * 1024 * 1024


def params_of():
    return pltpu.CompilerParams(vmem_limit_bytes=VMEM_BYTES)


def whole(*_):
    return pl.BlockSpec(memory_space=pltpu.VMEM)


def split2(values):
    high = values.astype(BF16)
    low = (values - high.astype(F32)).astype(BF16)
    return high, low


def split3(values):
    high = values.astype(BF16)
    rest = values - high.astype(F32)
    middle = rest.astype(BF16)
    low = (rest - middle.astype(F32)).astype(BF16)
    return high, middle, low


def gather_lanes(index_row, load_chunk, chunk_count):
    index = jnp.broadcast_to(index_row, (8, LANES))
    lane = index & (LANES - 1)
    chunk = index >> 7
    top = jnp.zeros((8, LANES), F32)
    bottom = jnp.zeros((8, LANES), F32)
    for c in range(chunk_count):
        block = load_chunk(c)
        here = chunk == c
        top = jnp.where(
            here, jnp.take_along_axis(block[:8], lane, axis=1, mode="promise_in_bounds"), top
        )
        bottom = jnp.where(
            here, jnp.take_along_axis(block[8:], lane, axis=1, mode="promise_in_bounds"), bottom
        )
    return jnp.concatenate([top, bottom], axis=0)


def send_kernel(index_ref, source_ref, out_ref):
    per = out_ref.shape[2] // LANES
    chunk_count = source_ref.shape[1] // LANES

    def step(j, carry):
        rows = gather_lanes(
            index_ref[pl.ds(j, 1), :],
            lambda c: source_ref[:, c * LANES : (c + 1) * LANES],
            chunk_count,
        )
        place = pl.multiple_of((j % per) * LANES, LANES)
        out_ref[j // per, :, pl.ds(place, LANES)] = rows
        return carry

    lax.fori_loop(0, index_ref.shape[0], step, 0)


def entry_kernel(index_ref, source_ref, out_ref):
    per = source_ref.shape[2] // LANES
    chunk_count = source_ref.shape[0] * per

    def step(j, carry):
        rows = gather_lanes(
            index_ref[pl.ds(j, 1), :],
            lambda c: source_ref[c // per, :, (c % per) * LANES : (c % per + 1) * LANES],
            chunk_count,
        )
        out_ref[:, pl.ds(pl.multiple_of(j * LANES, LANES), LANES)] = rows
        return carry

    lax.fori_loop(0, index_ref.shape[0], step, 0)


def one_tile(params, grads, length, centre_x, centre_y, before_ones, after_ones, moments):
    depth = params.shape[1]
    side = 16
    u = params[0:1] - centre_x
    v = params[1:2] - centre_y
    a = params[2:3]
    b = params[3:4]
    c = params[4:5]
    logit = params[5:6]
    local = lax.broadcasted_iota(jnp.int32, (side, depth), 0).astype(F32) - 7.5
    dx = local - u
    dy = local - v
    live = lax.broadcasted_iota(jnp.int32, (1, depth), 1) < length
    log_opacity = -(jnp.maximum(-logit, 0.0) + jnp.log(1.0 + jnp.exp(-jnp.abs(logit))))
    log_opacity = jnp.where(live, log_opacity * LOG2E, -1e30)
    part_x = (-0.5 * LOG2E) * (a * dx * dx)
    part_y = (-0.5 * LOG2E) * (c * dy * dy) + log_opacity
    cross = LOG2E * (b * dx)
    exponent = (part_x[None] + part_y[:, None]) - cross[None] * dy[:, None]
    exponent = exponent.reshape(side * side, depth)
    alpha = jnp.exp2(exponent)
    log_clear = jnp.log(1.0 - alpha) * LOG2E
    clear_high, clear_low = split2(log_clear)
    before = jnp.dot(clear_high, before_ones, preferred_element_type=F32) + jnp.dot(
        clear_low, before_ones, preferred_element_type=F32
    )
    weight = jnp.exp2(before) * alpha
    ratio = jnp.exp2(exponent - log_clear)
    grads_high, grads_low = split2(grads)
    colour_high, colour_low = split2(params[6:])
    pulled = lax.dot_general(
        jnp.concatenate([grads_high, grads_low, grads_high], axis=0),
        jnp.concatenate([colour_high, colour_high, colour_low], axis=0),
        (((0,), (0,)), ((), ())),
        preferred_element_type=F32,
    )
    flow = weight * pulled
    flow_high, flow_low = split2(flow)
    after = jnp.dot(flow_high, after_ones, preferred_element_type=F32) + jnp.dot(
        flow_low, after_ones, preferred_element_type=F32
    )
    change = flow - after * ratio
    weight_high, weight_low = split2(weight)
    colour_grads = (
        jnp.dot(grads_high, weight_high, preferred_element_type=F32)
        + jnp.dot(grads_low, weight_high, preferred_element_type=F32)
        + jnp.dot(grads_high, weight_low, preferred_element_type=F32)
    )
    sums = sum(jnp.dot(moments, piece, preferred_element_type=F32) for piece in split3(change))
    m00, m10, m01, m20, m02, m11 = (sums[i : i + 1] for i in range(6))
    sx = m10 - u * m00
    sy = m01 - v * m00
    sxx = m20 - 2.0 * u * m10 + u * u * m00
    syy = m02 - 2.0 * v * m01 + v * v * m00
    sxy = m11 - u * m01 - v * m10 + u * v * m00
    closed = 1.0 / (1.0 + jnp.exp(logit))
    return jnp.concatenate(
        [
            a * sx + b * sy,
            c * sy + b * sx,
            -0.5 * sxx,
            -sxy,
            -0.5 * syy,
            m00 * closed,
            colour_grads,
        ],
        axis=0,
    )


def tile_kernel(per_step, length_ref, params_ref, grads_ref, out_ref):
    depth = out_ref.shape[1] // per_step
    first = pl.program_id(0) * per_step
    row_base = lax.axis_index("narrow") * (pl.num_programs(0) * per_step)
    centre_x = (lax.axis_index("wide") * 16 + 8).astype(F32)
    low = lax.broadcasted_iota(jnp.int32, (depth, depth), 0)
    high = lax.broadcasted_iota(jnp.int32, (depth, depth), 1)
    before_ones = (low < high).astype(F32).astype(BF16)
    after_ones = (low > high).astype(F32).astype(BF16)
    pixel = lax.broadcasted_iota(jnp.int32, (8, 256), 1)
    which = lax.broadcasted_iota(jnp.int32, (8, 256), 0)
    x = (pixel & 15).astype(F32) - 7.5
    y = (pixel >> 4).astype(F32) - 7.5
    moments = jnp.where(which == 0, 1.0, 0.0)
    for i, term in enumerate((x, y, x * x, y * y, x * y)):
        moments = jnp.where(which == i + 1, term, moments)
    moments = moments.astype(BF16)
    for i in range(per_step):
        centre_y = ((row_base + first + i) * 16 + 8).astype(F32)
        out_ref[:, i * depth : (i + 1) * depth] = one_tile(
            params_ref[:, i * depth : (i + 1) * depth],
            grads_ref[i],
            length_ref[first + i],
            centre_x,
            centre_y,
            before_ones,
            after_ones,
            moments,
        )


GROUP = 16
STRIP = 256
ENTRY_BLOCK = 2048


def scatter_group(group, index_ref, load_values, out_store, spread_ref):
    entry_count = index_ref.shape[1]
    total = jnp.zeros((GROUP * 32, STRIP), F32)
    column = lax.broadcasted_iota(jnp.int32, (STRIP, ENTRY_BLOCK), 0)
    for block in range(entry_count // ENTRY_BLOCK):
        start = block * ENTRY_BLOCK
        index = index_ref[:, start : start + ENTRY_BLOCK]
        strip = index >> 8
        hot = jnp.where(column == (index & (STRIP - 1)), 1.0, 0.0).astype(BF16)
        high, low = split2(load_values(start))
        both = jnp.concatenate([high, low], axis=0)
        for c in range(GROUP):
            mask = jnp.where(strip == group * GROUP + c, 1.0, 0.0).astype(BF16)
            spread_ref[c * 32 : (c + 1) * 32, :] = both * mask
        total += lax.dot_general(
            spread_ref[...], hot, (((1,), (1,)), ((), ())), preferred_element_type=F32
        )
    for c in range(GROUP):
        out_store(c, total[c * 32 : c * 32 + 16] + total[c * 32 + 16 : c * 32 + 32])


def slot_kernel(index_ref, value_ref, out_ref, spread_ref):
    per = out_ref.shape[2] // LANES

    def store(group, c, rows):
        for part in range(STRIP // LANES):
            chunk = (group * GROUP + c) * (STRIP // LANES) + part
            place = (chunk % per) * LANES
            out_ref[chunk // per, :, place : place + LANES] = rows[
                :, part * LANES : (part + 1) * LANES
            ]

    strips = out_ref.shape[0] * out_ref.shape[2] // STRIP
    for group in range(strips // GROUP):
        scatter_group(
            group,
            index_ref,
            lambda start: value_ref[:, start : start + ENTRY_BLOCK],
            functools.partial(store, group),
            spread_ref,
        )


def splat_kernel(index_ref, value_ref, out_ref, spread_ref):
    cap = value_ref.shape[2]

    def load(start):
        if cap >= ENTRY_BLOCK:
            place = start % cap
            return value_ref[start // cap, :, place : place + ENTRY_BLOCK]
        return jnp.concatenate(
            [value_ref[start // cap + i] for i in range(ENTRY_BLOCK // cap)], axis=1
        )

    def store(c, rows):
        out_ref[:, c * STRIP : (c + 1) * STRIP] = rows

    scatter_group(pl.program_id(0), index_ref, load, store, spread_ref)


def body(splats, send_slots, tile_lists, tile_lengths, pixel_grads):
    features, local_count = splats.shape
    slot_count = send_slots.shape[2]
    tile_count, depth = tile_lists.shape[1:]
    entry_count = tile_count * depth
    columns = lax.axis_size("wide")
    cap = slot_count // columns
    sent_index = send_slots.reshape(slot_count // LANES, LANES)
    outgoing = pl.pallas_call(
        send_kernel,
        out_shape=jax.ShapeDtypeStruct((columns, features, cap), F32),
        in_specs=[whole(), whole()],
        out_specs=whole(),
        compiler_params=params_of(),
        name="send_gather",
    )(sent_index, splats)
    received = lax.all_to_all(outgoing, "wide", split_axis=0, concat_axis=0, tiled=True)
    all_params = pl.pallas_call(
        entry_kernel,
        out_shape=jax.ShapeDtypeStruct((features, entry_count), F32),
        in_specs=[whole(), whole()],
        out_specs=whole(),
        compiler_params=params_of(),
        name="entry_gather",
    )(tile_lists.reshape(entry_count // LANES, LANES), received)
    per_step = 2
    channels, pixels = pixel_grads.shape[0], pixel_grads.shape[3]
    grads_here = jnp.moveaxis(pixel_grads[:, 0], 1, 0)
    entry_grads = pl.pallas_call(
        functools.partial(tile_kernel, per_step),
        out_shape=jax.ShapeDtypeStruct((features, entry_count), F32),
        grid=(tile_count // per_step,),
        in_specs=[
            pl.BlockSpec(memory_space=pltpu.SMEM),
            pl.BlockSpec((features, per_step * depth), lambda i: (0, i)),
            pl.BlockSpec((per_step, channels, pixels), lambda i: (i, 0, 0)),
        ],
        out_specs=pl.BlockSpec((features, per_step * depth), lambda i: (0, i)),
        compiler_params=params_of(),
        name="tile_grads",
    )(tile_lengths.reshape(tile_count), all_params, grads_here)
    spread = pltpu.VMEM((GROUP * 32, ENTRY_BLOCK), BF16)
    slot_grads = pl.pallas_call(
        slot_kernel,
        out_shape=jax.ShapeDtypeStruct((columns, features, cap), F32),
        in_specs=[whole(), whole()],
        out_specs=whole(),
        scratch_shapes=[spread],
        compiler_params=params_of(),
        name="slot_scatter",
    )(tile_lists.reshape(1, entry_count), entry_grads)
    returned = lax.all_to_all(slot_grads, "wide", split_axis=0, concat_axis=0, tiled=True)
    partial_grads = pl.pallas_call(
        splat_kernel,
        out_shape=jax.ShapeDtypeStruct((features, local_count), F32),
        grid=(local_count // (GROUP * STRIP),),
        in_specs=[
            pl.BlockSpec((1, slot_count), lambda i: (0, 0)),
            pl.BlockSpec((columns, features, cap), lambda i: (0, 0, 0)),
        ],
        out_specs=pl.BlockSpec((features, GROUP * STRIP), lambda i: (0, i)),
        scratch_shapes=[spread],
        compiler_params=params_of(),
        name="splat_scatter",
    )(send_slots.reshape(1, slot_count), returned)
    other = lax.ppermute(partial_grads, "narrow", [(0, 1), (1, 0)])
    return partial_grads + other


def solution(mesh):
    placed = (
        P(None, ("groups", "wide")),
        P(("groups", "wide"), "narrow", None),
        P(("groups", "wide"), "narrow", None),
        P(("groups", "wide"), "narrow"),
        P(None, ("groups", "wide"), "narrow", None),
    )
    return jax.shard_map(
        body, mesh=mesh, in_specs=placed, out_specs=P(None, ("groups", "wide")), check_vma=False
    )
```

time: 420 us -> 124 us (0.30)
  local copies, waits for them, and re-layouts: 186 us -> 2.89 us
  other arithmetic: 110 us -> 1.08 us
  Pallas kernels: 0 us -> 76.6 us
  matrix products: 43.3 us -> 0 us
  waiting for transfers between devices: 38.1 us -> 16.9 us
  between operations: 13.6 us -> 0.09 us
    gather x6 -> x0, local copies, waits for them, and re-layouts: 99.5 us -> none  [the longest x2 33.9 us: body(): outgoing = jnp.take(splats, sent_index, axis=1)]
    pallas_call x0 -> x5, Pallas kernels: none -> 76.6 us  [the longest x1 22.7 us: body(): pl.pallas_call(send_kernel, out_shape=jax.ShapeDtypeStruct((columns, feat...]
    scatter-add x1 -> x0, other arithmetic: 48 us -> none  [body(): jnp.zeros((features, local_count), jnp.float32).at[:, sent_index]]
    dot_general x8 -> x0, matrix products: 43.3 us -> none  [tile_image(): jnp.einsum('bkp,cbk->cbp', weight, params[6:], precision=lax.Precision.HI...]
    psum x1 -> x0, waiting for transfers between devices: 38.1 us -> none  [body(): return lax.psum(partial_grads, 'narrow')]
    scatter x1 -> x0, local copies, waits for them, and re-layouts: 30.5 us -> none  [body(): slot_source = jnp.full((slot_count,), entry_count, jnp.int32).at[live_tar...]
    another operation x24 -> x0, other arithmetic: 29.1 us -> none
    reduce_sum x4 -> x0, other arithmetic: 27.3 us -> none  [tile_image(): params[3][:, :, None] * delta_x * delta_y]
  transfers between devices with their start and end apart: 2 -> 2, of which waited for: 1 -> 2; matrix products, arithmetic and copies ran while one was open for 8% -> 0% of each run, Pallas kernels for 0% -> 0%
where the time goes in v1:
time: 124 us; the launch traced here: 123 us
  Pallas kernels  76.6 us (62%)
  blocking collectives  18.2 us (15%)
  waiting for transfers between devices  16.9 us (14%)
  starting transfers between devices  7.48 us (6%)
  local copies, waits for them, and re-layouts  2.89 us (2%)
    pallas_call x1, Pallas kernels, body(): pl.pallas_call(send_kernel, out_shape=jax.ShapeDtypeStruct((columns, feat...  22.7 us
    pallas_call x1, Pallas kernels, body(): pl.pallas_call(functools.partial(tile_kernel, per_step), out_shape=jax.Sh...  22 us
    all_to_all x1, blocking collectives, body(): lax.all_to_all(slot_grads, 'wide', split_axis=0, concat_axis=0, tiled=True)  18.2 us
    all_to_all x1, waiting for transfers between devices, body(): lax.all_to_all(outgoing, 'wide', split_axis=0, concat_axis=0, tiled=True)  14.2 us
    pallas_call x1, Pallas kernels, body(): pl.pallas_call(entry_kernel, out_shape=jax.ShapeDtypeStruct((features, en...  13.2 us
    pallas_call x1, Pallas kernels, body(): pl.pallas_call(splat_kernel, out_shape=jax.ShapeDtypeStruct((features, lo...  12.8 us
    all_to_all x1, starting transfers between devices, body(): lax.all_to_all(outgoing, 'wide', split_axis=0, concat_axis=0, tiled=True)  7.41 us
    pallas_call x1, Pallas kernels, body(): pl.pallas_call(slot_kernel, out_shape=jax.ShapeDtypeStruct((columns, feat...  5.82 us
  transfers between devices with their start and end apart: 2, of which 2 were waited for; matrix products, arithmetic and copies ran while one was open for 0% of the time, Pallas kernels for 0%

profile of v1, /device:TPU:0, one launch (start us, length us, event | category | flops | bytes accessed | tf_op | source)
XLA Modules:
  0.0 123.2 jit_solution(13209810433750212536)
XLA Ops:
  0.0 0.0 copy-start
  0.0 1.2 copy-done
  1.2 0.0 copy-start.1
  1.2 0.8 copy-done.1
  2.0 22.7 %send_gather.1 = f32[8,16,1024]{2,1,0:T(8,128)} custom-call(s32[64,128]{1,0:T(8,128)S(1)} %bitcast.11, f32[16,16384]{1,0:T(8,128)S(1)} %copy-done), custom_call_target="tpu_custom_call" | custom-call | tf_op jit(solution)/shard_map/send_gather/pallas_call | solution.py:265
  24.7 0.0 copy-start.5
  24.7 0.0 copy-start.4
  24.7 7.4 %all-to-all-start = ((f32[8,16,1024]{2,1,0:T(8,128)}), f32[8,16,1024]{2,1,0:T(8,128)S(1)}, u32[]{:S(2)}, u32[]{:S(2)}) async-start(f32[8,16,1024]{2,1,0:T(8,128)} %send_gather.1), calls=%async_computation | async-start | bytes 1048576 | tf_op jit(solution)/shard_map/all_to_all | solution.py:273
  32.1 0.0 copy-done.5
  32.1 0.0 copy-done.4
  32.1 0.2 copy.9
  32.4 14.2 %all-to-all-done.source_ref = f32[8,16,1024]{2,1,0:T(8,128)S(1)} async-done(((f32[8,16,1024]{2,1,0:T(8,128)}), f32[8,16,1024]{2,1,0:T(8,128)S(1)}, u32[]{:S(2)}, u32[]{:S(2)}) %all-to-all-start) | async-done | bytes 524320 | tf_op jit(solution)/shard_map/all_to_all | solution.py:273
  46.6 13.2 %entry_gather.1.params_ref = f32[16,8192]{1,0:T(8,128)S(1)} custom-call(s32[64,128]{1,0:T(8,128)S(1)} %reshape.18.index_ref, f32[8,16,1024]{2,1,0:T(8,128)S(1)} %all-to-all-done.source_ref), custom_call_target="tpu_custom_call" | custom-call | tf_op jit(solution)/shard_map/entry_gather/pallas_call | solution.py:274
  59.8 0.0 copy-start.3
  59.8 0.6 copy-done.3
  60.5 22.0 %tile_grads.1.value_ref = f32[16,8192]{1,0:T(8,128)S(1)} custom-call(s32[32]{0:T(128)S(1)} %bitcast.14, f32[16,8192]{1,0:T(8,128)S(1)} %entry_gather.1.params_ref, f32[32,10,256]{2,1,0:T(8,128)S(1)} %bitcast.10), custom_call_target="tpu_custom_call" | custom-call | tf_op jit(solution)/shard_map/tile_grads/pallas_call | solution.py:285
  82.4 5.8 %slot_scatter.1 = f32[8,16,1024]{2,1,0:T(8,128)S(1)} custom-call(s32[1,8192]{1,0:T(1,128)S(1)} %bitcast.13, f32[16,8192]{1,0:T(8,128)S(1)} %tile_grads.1.value_ref), custom_call_target="tpu_custom_call" | custom-call | tf_op jit(solution)/shard_map/slot_scatter/pallas_call | solution.py:299
  88.3 0.0 copy-start.2
  88.3 18.2 %all_to_all.10.value_ref = f32[8,16,1024]{2,1,0:T(8,128)S(1)} all-to-all(f32[8,16,1024]{2,1,0:T(8,128)S(1)} %slot_scatter.1), channel_id=1, replica_groups=mesh['groups'=2,'wide'=8,'narrow'=2] {'wide'}, dimensions={0} | all-to-all | bytes 1048576 | tf_op jit(solution)/shard_map/all_to_all | solution.py:308
  106.5 0.0 copy-done.2
  106.5 12.8 %splat_scatter.1 = f32[16,16384]{1,0:T(8,128)S(1)} custom-call(s32[1,8192]{1,0:T(1,128)S(1)} %bitcast.12, f32[8,16,1024]{2,1,0:T(8,128)S(1)} %all_to_all.10.value_ref), custom_call_target="tpu_custom_call" | custom-call | tf_op jit(solution)/shard_map/splat_scatter/pallas_call | solution.py:309
  119.4 0.1 collective-permute-start
  119.4 2.6 %collective-permute-done = f32[16,16384]{1,0:T(8,128)S(1)} collective-permute-done((f32[16,16384]{1,0:T(8,128)S(1)}, f32[16,16384]{1,0:T(8,128)S(1)}, u32[]{:S(2)}, u32[]{:S(2)}) %collective-permute-start) | collective-permute-done | bytes 1048608 | tf_op jit(solution)/shard_map/ppermute | solution.py:322
  122.1 1.1 add.3
  (2 shorter events, 0.0 us)
Async XLA Ops:
  0.0 1.2 copy-start
  1.2 0.8 copy-start.1
  24.7 7.4 %copy-start.5 = (s32[1,32,256]{2,1,0:T(8,128)S(1)}, s32[1,32,256]{2,1,0:T(8,128)}, u32[]{:S(2)}) copy-start(s32[1,32,256]{2,1,0:T(8,128)} %param.7) | copy-start | bytes 98308
  24.7 7.5 %copy-start.4 = (f32[10,1,32,256]{3,2,1,0:T(8,128)S(1)}, f32[10,1,32,256]{3,2,1,0:T(8,128)}, u32[]{:S(2)}) copy-start(f32[10,1,32,256]{3,2,1,0:T(8,128)} %param.9) | copy-start | bytes 983044
  24.7 21.9 %all-to-all-start = ((f32[8,16,1024]{2,1,0:T(8,128)}), f32[8,16,1024]{2,1,0:T(8,128)S(1)}, u32[]{:S(2)}, u32[]{:S(2)}) async-start(f32[8,16,1024]{2,1,0:T(8,128)} %send_gather.1), calls=%async_computation | async-start | bytes 1048576 | tf_op jit(solution)/shard_map/all_to_all | solution.py:273
  59.8 0.7 copy-start.3
  88.3 18.2 %copy-start.2 = (s32[1,1,8192]{2,1,0:T(1,128)S(1)}, s32[1,1,8192]{2,1,0:T(1,128)}, u32[]{:S(2)}) copy-start(s32[1,1,8192]{2,1,0:T(1,128)} %param.6) | copy-start | bytes 98308
  119.4 2.7 %collective-permute-start = (f32[16,16384]{1,0:T(8,128)S(1)}, f32[16,16384]{1,0:T(8,128)S(1)}, u32[]{:S(2)}, u32[]{:S(2)}) collective-permute-start(f32[16,16384]{1,0:T(8,128)S(1)} %splat_scatter.1), channel_id=1, source_target_pairs={{0,1},{1,0},{2,3},{3,2},{4,5},{5,4},{6,7},{7,6},{8,9},{9,8},{10,11... | collective-permute-start | bytes 3145736 | tf_op jit(solution)/shard_map/ppermute | solution.py:322

commit v2 on v1

--- a/solution.py
+++ b/solution.py
@@ -37,55 +37,147 @@
     return high, middle, low
 
 
-def gather_lanes(index_row, load_chunk, chunk_count):
-    index = jnp.broadcast_to(index_row, (8, LANES))
-    lane = index & (LANES - 1)
-    chunk = index >> 7
-    top = jnp.zeros((8, LANES), F32)
-    bottom = jnp.zeros((8, LANES), F32)
-    for c in range(chunk_count):
-        block = load_chunk(c)
-        here = chunk == c
-        top = jnp.where(
-            here, jnp.take_along_axis(block[:8], lane, axis=1, mode="promise_in_bounds"), top
+STRIP = 256
+PAIR_ROWS = 80
+PAIRS_PER_DOT = 8
+MESH = pl.DeviceIdType.MESH
+
+
+def spread_pair(first_strip, second_strip):
+    first = split3(first_strip)
+    second = split3(second_strip)
+    low = jnp.concatenate([first[2].astype(F32)[:8], second[2].astype(F32)[:8]], axis=0)
+    return jnp.concatenate([first[0], first[1], second[0], second[1], low.astype(BF16)], axis=0)
+
+
+def gather_strip(index, spread_ref, first_pair, pair_count, strip_of):
+    width = spread_ref.shape[1]
+    count = index.shape[1]
+    strip = jnp.broadcast_to(index // width, (8, count))
+    column = lax.broadcasted_iota(jnp.int32, (width, count), 0)
+    hot = jnp.where(column == (index & (width - 1)), 1.0, 0.0).astype(BF16)
+    parts = [jnp.zeros((8, count), F32) for _ in range(5)]
+    per_dot = min(PAIRS_PER_DOT, pair_count)
+    rows = per_dot * PAIR_ROWS
+    for block in range(pair_count // per_dot):
+        start_row = first_pair * PAIR_ROWS + block * rows
+        found = jnp.dot(
+            spread_ref[start_row : start_row + rows, :], hot, preferred_element_type=F32
         )
-        bottom = jnp.where(
-            here, jnp.take_along_axis(block[8:], lane, axis=1, mode="promise_in_bounds"), bottom
+        for p in range(per_dot):
+            for q in range(2):
+                here = strip == strip_of((first_pair + block * per_dot + p) * 2 + q)
+                base = p * PAIR_ROWS
+                starts = [base + q * 32 + 8 * i for i in range(4)] + [base + 64 + 8 * q]
+                parts = [
+                    jnp.where(here, found[start : start + 8], part)
+                    for start, part in zip(starts, parts)
+                ]
+    return jnp.concatenate([parts[0] + (parts[2] + parts[4]), parts[1] + parts[3]], axis=0)
+
+
+def copy_between(send_ref, recv_ref, send_sems, recv_sems, peer, mine):
+    return pltpu.make_async_remote_copy(
+        src_ref=send_ref.at[peer],
+        dst_ref=recv_ref.at[mine],
+        send_sem=send_sems.at[peer],
+        recv_sem=recv_sems.at[mine],
+        device_id={"wide": peer},
+        device_id_type=MESH,
+    )
+
+
+def greet(columns, me):
+    barrier = pltpu.get_barrier_semaphore()
+
+    def hello(step, carry):
+        peer = lax.rem(me + 1 + step, columns)
+        pl.semaphore_signal(barrier, inc=1, device_id={"wide": peer}, device_id_type=MESH)
+        return carry
+
+    lax.fori_loop(0, columns - 1, hello, 0)
+    return barrier
+
+
+def wait_sends(columns, me, send_ref, recv_ref, send_sems, recv_sems):
+    def done(step, carry):
+        peer = lax.rem(me + 1 + step, columns)
+        copy_between(send_ref, recv_ref, send_sems, recv_sems, peer, me).wait_send()
+        return carry
+
+    lax.fori_loop(0, columns - 1, done, 0)
+
+
+def offset_of(step, columns):
+    away = (step + 1) // 2
+    return columns // 2 + away * (1 - 2 * (step % 2))
+
+
+def receive_kernel(
+    sent_ref, source_ref, list_ref, out_ref,
+    spread_ref, spread_recv_ref, send_ref, recv_ref, send_sems, recv_sems,
+):
+    columns, _, cap = recv_ref.shape
+    me = lax.axis_index("wide")
+    barrier = greet(columns, me)
+    source_strips = source_ref.shape[1] // STRIP
+    for p in range(source_strips // 2):
+        start = p * 2 * STRIP
+        spread_ref[p * PAIR_ROWS : (p + 1) * PAIR_ROWS, :] = spread_pair(
+            source_ref[:, start : start + STRIP], source_ref[:, start + STRIP : start + 2 * STRIP]
         )
-    return jnp.concatenate([top, bottom], axis=0)
-
-
-def send_kernel(index_ref, source_ref, out_ref):
-    per = out_ref.shape[2] // LANES
-    chunk_count = source_ref.shape[1] // LANES
-
-    def step(j, carry):
-        rows = gather_lanes(
-            index_ref[pl.ds(j, 1), :],
-            lambda c: source_ref[:, c * LANES : (c + 1) * LANES],
-            chunk_count,
-        )
-        place = pl.multiple_of((j % per) * LANES, LANES)
-        out_ref[j // per, :, pl.ds(place, LANES)] = rows
+    pl.semaphore_wait(barrier, columns - 1)
+    width = sent_ref.shape[1]
+    per = cap // width
+
+    def pick(peer, place):
+        index = sent_ref[pl.ds(peer * per + place, 1), :]
+        return gather_strip(index, spread_ref, 0, source_strips // 2, lambda strip: strip)
+
+    def send(step, carry):
+        peer = lax.rem(me + offset_of(step, columns), columns)
+        for i in range(per):
+            send_ref[peer, :, i * width : (i + 1) * width] = pick(peer, i)
+        copy_between(send_ref, recv_ref, send_sems, recv_sems, peer, me).start()
         return carry
 
-    lax.fori_loop(0, index_ref.shape[0], step, 0)
-
-
-def entry_kernel(index_ref, source_ref, out_ref):
-    per = source_ref.shape[2] // LANES
-    chunk_count = source_ref.shape[0] * per
-
-    def step(j, carry):
-        rows = gather_lanes(
-            index_ref[pl.ds(j, 1), :],
-            lambda c: source_ref[c // per, :, (c % per) * LANES : (c % per + 1) * LANES],
-            chunk_count,
-        )
-        out_ref[:, pl.ds(pl.multiple_of(j * LANES, LANES), LANES)] = rows
-        return carry
-
-    lax.fori_loop(0, index_ref.shape[0], step, 0)
+    lax.fori_loop(0, columns - 1, send, 0)
+    for i in range(per):
+        recv_ref[me, :, i * width : (i + 1) * width] = pick(me, i)
+
+    half = columns // 2
+    strips_half = half * per
+    pairs_half = strips_half // 2
+    sources = [lax.rem(me + columns - offset_of(k, columns), columns) for k in range(columns)]
+    for phase in range(2):
+        for k in range(phase * half, (phase + 1) * half):
+            if k < columns - 1:
+                copy_between(send_ref, recv_ref, send_sems, recv_sems, sources[k], sources[k]).wait_recv()
+        strips = [
+            (sources[phase * half + i // per], (i % per) * width) for i in range(strips_half)
+        ]
+        for p in range(pairs_half):
+            blocks = [
+                recv_ref[source, :, place : place + width]
+                for source, place in strips[2 * p : 2 * p + 2]
+            ]
+            row = (phase * pairs_half + p) * PAIR_ROWS
+            spread_recv_ref[row : row + PAIR_ROWS, :] = spread_pair(*blocks)
+
+        def step(j, carry):
+            found = gather_strip(
+                list_ref[pl.ds(j, 1), :],
+                spread_recv_ref,
+                phase * pairs_half,
+                pairs_half,
+                lambda strip: sources[strip // per] * per + strip % per,
+            )
+            where = pl.ds(pl.multiple_of(j * STRIP, STRIP), STRIP)
+            out_ref[:, where] = found if phase == 0 else out_ref[:, where] + found
+            return carry
+
+        lax.fori_loop(0, list_ref.shape[0], step, 0, unroll=2)
+    wait_sends(columns, me, send_ref, recv_ref, send_sems, recv_sems)
 
 
 def one_tile(params, grads, length, centre_x, centre_y, before_ones, after_ones, moments):
@@ -190,20 +282,17 @@
 
 
 GROUP = 16
-STRIP = 256
 ENTRY_BLOCK = 2048
 
 
-def scatter_group(group, index_ref, load_values, out_store, spread_ref):
-    entry_count = index_ref.shape[1]
+def scatter_group(group, blocks, spread_ref):
     total = jnp.zeros((GROUP * 32, STRIP), F32)
     column = lax.broadcasted_iota(jnp.int32, (STRIP, ENTRY_BLOCK), 0)
-    for block in range(entry_count // ENTRY_BLOCK):
-        start = block * ENTRY_BLOCK
-        index = index_ref[:, start : start + ENTRY_BLOCK]
+    for load_index, load_values in blocks:
+        index = load_index()
         strip = index >> 8
         hot = jnp.where(column == (index & (STRIP - 1)), 1.0, 0.0).astype(BF16)
-        high, low = split2(load_values(start))
+        high, low = split2(load_values())
         both = jnp.concatenate([high, low], axis=0)
         for c in range(GROUP):
             mask = jnp.where(strip == group * GROUP + c, 1.0, 0.0).astype(BF16)
@@ -211,47 +300,80 @@
         total += lax.dot_general(
             spread_ref[...], hot, (((1,), (1,)), ((), ())), preferred_element_type=F32
         )
-    for c in range(GROUP):
-        out_store(c, total[c * 32 : c * 32 + 16] + total[c * 32 + 16 : c * 32 + 32])
-
-
-def slot_kernel(index_ref, value_ref, out_ref, spread_ref):
-    per = out_ref.shape[2] // LANES
-
-    def store(group, c, rows):
-        for part in range(STRIP // LANES):
-            chunk = (group * GROUP + c) * (STRIP // LANES) + part
-            place = (chunk % per) * LANES
-            out_ref[chunk // per, :, place : place + LANES] = rows[
-                :, part * LANES : (part + 1) * LANES
-            ]
-
-    strips = out_ref.shape[0] * out_ref.shape[2] // STRIP
-    for group in range(strips // GROUP):
-        scatter_group(
-            group,
-            index_ref,
-            lambda start: value_ref[:, start : start + ENTRY_BLOCK],
-            functools.partial(store, group),
-            spread_ref,
+    return [
+        total[c * 32 : c * 32 + 16] + total[c * 32 + 16 : c * 32 + 32] for c in range(GROUP)
+    ]
+
+
+def return_kernel(
+    list_ref, value_ref, sent_ref, out_ref, spread_ref, send_ref, recv_ref, send_sems, recv_sems
+):
+    columns, _, cap = recv_ref.shape
+    me = lax.axis_index("wide")
+    barrier = greet(columns, me)
+    half = columns // 2
+    my_half = me // half
+    entry_blocks = [
+        (
+            lambda start=start: list_ref[:, start : start + ENTRY_BLOCK],
+            lambda start=start: value_ref[:, start : start + ENTRY_BLOCK],
         )
-
-
-def splat_kernel(index_ref, value_ref, out_ref, spread_ref):
-    cap = value_ref.shape[2]
-
-    def load(start):
-        if cap >= ENTRY_BLOCK:
-            place = start % cap
-            return value_ref[start // cap, :, place : place + ENTRY_BLOCK]
-        return jnp.concatenate(
-            [value_ref[start // cap + i] for i in range(ENTRY_BLOCK // cap)], axis=1
-        )
-
-    def store(c, rows):
-        out_ref[:, c * STRIP : (c + 1) * STRIP] = rows
-
-    scatter_group(pl.program_id(0), index_ref, load, store, spread_ref)
+        for start in range(0, list_ref.shape[1], ENTRY_BLOCK)
+    ]
+    for phase in range(2):
+        group = my_half if phase else 1 - my_half
+        strips = scatter_group(group, entry_blocks, spread_ref)
+        for c, rows in enumerate(strips):
+            for part in range(STRIP // LANES):
+                start = c * STRIP + part * LANES
+                place = start % cap
+                send_ref[group * half + start // cap, :, place : place + LANES] = rows[
+                    :, part * LANES : (part + 1) * LANES
+                ]
+        if phase == 0:
+            pl.semaphore_wait(barrier, columns - 1)
+
+        def send(step, carry):
+            peer = group * half + lax.rem(me + step, half)
+            copy_between(send_ref, recv_ref, send_sems, recv_sems, peer, me).start()
+            return carry
+
+        lax.fori_loop(phase, half, send, 0)
+    recv_ref[me] = send_ref[me]
+
+    per_block = ENTRY_BLOCK // cap
+    for phase in range(2):
+        from_half = my_half if phase else 1 - my_half
+
+        def arrived(step, carry):
+            source = from_half * half + lax.rem(me + step, half)
+            copy_between(send_ref, recv_ref, send_sems, recv_sems, source, source).wait_recv()
+            return carry
+
+        lax.fori_loop(phase, half, arrived, 0)
+        blocks = []
+        for block in range(half // per_block):
+            first = from_half * half + block * per_block
+            blocks.append(
+                (
+                    lambda first=first: sent_ref[
+                        :, pl.ds(pl.multiple_of(first * cap, LANES), ENTRY_BLOCK)
+                    ],
+                    lambda first=first: jnp.concatenate(
+                        [recv_ref[first + i] for i in range(per_block)], axis=1
+                    ),
+                )
+            )
+
+        def splat_group(group, carry):
+            found = scatter_group(group, blocks, spread_ref)
+            for c, rows in enumerate(found):
+                where = pl.ds(pl.multiple_of((group * GROUP + c) * STRIP, STRIP), STRIP)
+                out_ref[:, where] = rows if phase == 0 else out_ref[:, where] + rows
+            return carry
+
+        lax.fori_loop(0, out_ref.shape[1] // (GROUP * STRIP), splat_group, 0)
+    wait_sends(columns, me, send_ref, recv_ref, send_sems, recv_sems)
 
 
 def body(splats, send_slots, tile_lists, tile_lengths, pixel_grads):
@@ -261,24 +383,32 @@
     entry_count = tile_count * depth
     columns = lax.axis_size("wide")
     cap = slot_count // columns
-    sent_index = send_slots.reshape(slot_count // LANES, LANES)
-    outgoing = pl.pallas_call(
-        send_kernel,
-        out_shape=jax.ShapeDtypeStruct((columns, features, cap), F32),
-        in_specs=[whole(), whole()],
+    width = min(cap, STRIP)
+    exchange = [
+        pltpu.VMEM((columns, features, cap), F32),
+        pltpu.VMEM((columns, features, cap), F32),
+        pltpu.SemaphoreType.DMA((columns,)),
+        pltpu.SemaphoreType.DMA((columns,)),
+    ]
+    all_params = pl.pallas_call(
+        receive_kernel,
+        out_shape=jax.ShapeDtypeStruct((features, entry_count), F32),
+        in_specs=[whole(), whole(), whole()],
         out_specs=whole(),
-        compiler_params=params_of(),
-        name="send_gather",
-    )(sent_index, splats)
-    received = lax.all_to_all(outgoing, "wide", split_axis=0, concat_axis=0, tiled=True)
-    all_params = pl.pallas_call(
-        entry_kernel,
-        out_shape=jax.ShapeDtypeStruct((features, entry_count), F32),
-        in_specs=[whole(), whole()],
-        out_specs=whole(),
-        compiler_params=params_of(),
-        name="entry_gather",
-    )(tile_lists.reshape(entry_count // LANES, LANES), received)
+        scratch_shapes=[
+            pltpu.VMEM((local_count // STRIP // 2 * PAIR_ROWS, STRIP), BF16),
+            pltpu.VMEM((slot_count // width // 2 * PAIR_ROWS, width), BF16),
+        ]
+        + exchange,
+        compiler_params=pltpu.CompilerParams(
+            vmem_limit_bytes=VMEM_BYTES, collective_id=0, has_side_effects=True
+        ),
+        name="receive_entries",
+    )(
+        send_slots.reshape(slot_count // width, width),
+        splats,
+        tile_lists.reshape(entry_count // STRIP, STRIP),
+    )
     per_step = 2
     channels, pixels = pixel_grads.shape[0], pixel_grads.shape[3]
     grads_here = jnp.moveaxis(pixel_grads[:, 0], 1, 0)
@@ -295,30 +425,21 @@
         compiler_params=params_of(),
         name="tile_grads",
     )(tile_lengths.reshape(tile_count), all_params, grads_here)
-    spread = pltpu.VMEM((GROUP * 32, ENTRY_BLOCK), BF16)
-    slot_grads = pl.pallas_call(
-        slot_kernel,
-        out_shape=jax.ShapeDtypeStruct((columns, features, cap), F32),
-        in_specs=[whole(), whole()],
+    partial_grads = pl.pallas_call(
+        return_kernel,
+        out_shape=jax.ShapeDtypeStruct((features, local_count), F32),
+        in_specs=[whole(), whole(), whole()],
         out_specs=whole(),
-        scratch_shapes=[spread],
-        compiler_params=params_of(),
-        name="slot_scatter",
-    )(tile_lists.reshape(1, entry_count), entry_grads)
-    returned = lax.all_to_all(slot_grads, "wide", split_axis=0, concat_axis=0, tiled=True)
-    partial_grads = pl.pallas_call(
-        splat_kernel,
-        out_shape=jax.ShapeDtypeStruct((features, local_count), F32),
-        grid=(local_count // (GROUP * STRIP),),
-        in_specs=[
-            pl.BlockSpec((1, slot_count), lambda i: (0, 0)),
-            pl.BlockSpec((columns, features, cap), lambda i: (0, 0, 0)),
-        ],
-        out_specs=pl.BlockSpec((features, GROUP * STRIP), lambda i: (0, i)),
-        scratch_shapes=[spread],
-        compiler_params=params_of(),
-        name="splat_scatter",
-    )(send_slots.reshape(1, slot_count), returned)
+        scratch_shapes=[pltpu.VMEM((GROUP * 32, ENTRY_BLOCK), BF16)] + exchange,
+        compiler_params=pltpu.CompilerParams(
+            vmem_limit_bytes=VMEM_BYTES, collective_id=1, has_side_effects=True
+        ),
+        name="return_grads",
+    )(
+        tile_lists.reshape(1, entry_count),
+        entry_grads,
+        send_slots.reshape(1, slot_count),
+    )
     other = lax.ppermute(partial_grads, "narrow", [(0, 1), (1, 0)])
     return partial_grads + other
 

time: 124 us -> 93.9 us (0.76)
  blocking collectives: 18.2 us -> 0 us
  waiting for transfers between devices: 16.9 us -> 2.65 us
  Pallas kernels: 76.6 us -> 84.3 us
  starting transfers between devices: 7.48 us -> 0.07 us
  other arithmetic: 1.08 us -> 2.55 us
    all_to_all x1 -> x0, blocking collectives: 18.2 us -> none  [body(): lax.all_to_all(slot_grads, 'wide', split_axis=0, concat_axis=0, tiled=True)]
    all_to_all x1 -> x0, waiting for transfers between devices: 14.2 us -> none  [body(): lax.all_to_all(outgoing, 'wide', split_axis=0, concat_axis=0, tiled=True)]
    pallas_call x4 -> x2, Pallas kernels: 54.6 us -> 62.3 us  [the longest x1 31.8 us: body(): pl.pallas_call(return_kernel, out_shape=jax.ShapeDtypeStruct((features, l...]
    all_to_all x1 -> x0, starting transfers between devices: 7.41 us -> none  [body(): lax.all_to_all(outgoing, 'wide', split_axis=0, concat_axis=0, tiled=True)]
    unnamed x0 -> x1, other arithmetic: none -> 1.48 us
    unnamed x14 -> x11, local copies, waits for them, and re-layouts: 2.88 us -> 3.89 us
  transfers between devices with their start and end apart: 2 -> 1, of which waited for: 2 -> 1; matrix products, arithmetic and copies ran while one was open for 0% -> 0% of each run, Pallas kernels for 0% -> 0%
where the time goes in v2:
time: 93.9 us; the launch traced here: 93.6 us
  Pallas kernels  84.3 us (90%)
  local copies, waits for them, and re-layouts  3.9 us (4%)
  waiting for transfers between devices  2.65 us (3%)
  other arithmetic  2.55 us (3%)
    pallas_call x1, Pallas kernels, body(): pl.pallas_call(return_kernel, out_shape=jax.ShapeDtypeStruct((features, l...  31.8 us
    pallas_call x1, Pallas kernels, body(): pl.pallas_call(receive_kernel, out_shape=jax.ShapeDtypeStruct((features,...  30.6 us
    pallas_call x1, Pallas kernels, body(): pl.pallas_call(functools.partial(tile_kernel, per_step), out_shape=jax.Sh...  22 us
    unnamed x11, local copies, waits for them, and re-layouts  3.89 us
    ppermute x1, waiting for transfers between devices, body(): other = lax.ppermute(partial_grads, 'narrow', [(0, 1), (1, 0)])  2.65 us
  transfers between devices with their start and end apart: 1, of which 1 were waited for; matrix products, arithmetic and copies ran while one was open for 0% of the time, Pallas kernels for 0%

profile of v2, /device:TPU:0, one launch (start us, length us, event | category | flops | bytes accessed | tf_op | source)
XLA Modules:
  0.0 93.6 jit_solution(5790023629802852929)
XLA Ops:
  0.0 0.0 copy-start
  0.0 0.5 broadcast.3
  0.5 1.5 %reduce.3 = s32[8192]{0:T(1024)S(1)} reduce(s32[1,1,8192]{2,1,0:T(1,128)} %param.6, s32[]{:T(128)} %broadcast.3), dimensions={0,1}, to_apply=%param.6.reduce_sub_computation.3 | reduce | bytes 65540 | tf_op args[1]
  2.0 0.8 copy.7
  2.8 1.2 %copy.9 = f32[10,1,32,256]{3,0,2,1:T(8,128)S(1)} copy(f32[10,1,32,256]{3,2,1,0:T(8,128)} %param.9) | data formatting | bytes 655360 | tf_op args[4]
  4.0 0.0 copy-done
  4.0 0.0 copy-start.1
  4.0 0.7 copy-done.1
  4.8 30.6 %receive_entries.1.params_ref = f32[16,8192]{1,0:T(8,128)S(1)} custom-call(s32[32,256]{1,0:T(8,128)S(1)} %reshape.17.sent_ref, f32[16,16384]{1,0:T(8,128)S(1)} %copy-done, s32[32,256]{1,0:T(8,128)S(1)} %bitcast.12), custom_call_target="tpu_custom_call" | custom-call | tf_op jit(solution)/shard_map/receive_entries/pallas_call | solution.py:393
  35.3 0.0 copy-start.3
  35.3 0.6 copy-done.3
  36.0 0.0 copy-start.2
  36.0 22.0 %tile_grads.1.value_ref = f32[16,8192]{1,0:T(8,128)S(1)} custom-call(s32[32]{0:T(128)S(1)} %bitcast.15, f32[16,8192]{1,0:T(8,128)S(1)} %receive_entries.1.params_ref, f32[32,10,256]{2,1,0:T(8,128)S(1)} %bitcast.10), custom_call_target="tpu_custom_call" | custom-call | tf_op jit(solution)/shard_map/tile_grads/pallas_call | solution.py:415
  58.0 0.0 copy-done.2
  58.0 31.8 %return_grads.1 = f32[16,16384]{1,0:T(8,128)S(1)} custom-call(s32[1,8192]{1,0:T(1,128)S(1)} %bitcast.14, f32[16,8192]{1,0:T(8,128)S(1)} %tile_grads.1.value_ref, s32[1,8192]{1,0:T(1,128)S(1)} %bitcast.13), custom_call_target="tpu_custom_call" | custom-call | tf_op jit(solution)/shard_map/return_grads/pallas_call | solution.py:428
  89.7 0.1 collective-permute-start
  89.8 2.6 %collective-permute-done = f32[16,16384]{1,0:T(8,128)S(1)} collective-permute-done((f32[16,16384]{1,0:T(8,128)S(1)}, f32[16,16384]{1,0:T(8,128)S(1)}, u32[]{:S(2)}, u32[]{:S(2)}) %collective-permute-start) | collective-permute-done | bytes 1048608 | tf_op jit(solution)/shard_map/ppermute | solution.py:443
  92.5 1.1 %add.3 = f32[16,16384]{1,0:T(8,128)} add(f32[16,16384]{1,0:T(8,128)S(1)} %return_grads.1, f32[16,16384]{1,0:T(8,128)S(1)} %collective-permute-done) | non-fusion elementwise | flops 262144 | bytes 3145728 | tf_op jit(solution)/shard_map/add | solution.py:444
  (1 shorter events, 0.0 us)
Async XLA Ops:
  0.0 4.0 %copy-start = (f32[16,16384]{1,0:T(8,128)S(1)}, f32[16,16384]{1,0:T(8,128)}, u32[]{:S(2)}) copy-start(f32[16,16384]{1,0:T(8,128)} %source_ref.1) | copy-start | bytes 3145732
  4.0 0.8 copy-start.1
  35.3 0.7 copy-start.3
  36.0 22.0 %copy-start.2 = (s32[1,1,8192]{2,1,0:T(1,128)S(1)}, s32[1,1,8192]{2,1,0:T(1,128)}, u32[]{:S(2)}) copy-start(s32[1,1,8192]{2,1,0:T(1,128)} %param.6) | copy-start | bytes 98308
  89.7 2.7 %collective-permute-start = (f32[16,16384]{1,0:T(8,128)S(1)}, f32[16,16384]{1,0:T(8,128)S(1)}, u32[]{:S(2)}, u32[]{:S(2)}) collective-permute-start(f32[16,16384]{1,0:T(8,128)S(1)} %return_grads.1), channel_id=1, source_target_pairs={{0,1},{1,0},{2,3},{3,2},{4,5},{5,4},{6,7},{7,6},{8,9},{9,8},{10,11... | collective-permute-start | bytes 3145736 | tf_op jit(solution)/shard_map/ppermute | solution.py:443

commit v3 on v2

--- a/solution.py
+++ b/solution.py
@@ -39,7 +39,7 @@
 
 STRIP = 256
 PAIR_ROWS = 80
-PAIRS_PER_DOT = 8
+PAIRS_PER_DOT = 2
 MESH = pl.DeviceIdType.MESH
 
 
@@ -127,11 +127,12 @@
             source_ref[:, start : start + STRIP], source_ref[:, start + STRIP : start + 2 * STRIP]
         )
     pl.semaphore_wait(barrier, columns - 1)
-    width = sent_ref.shape[1]
+    width = min(cap, STRIP)
     per = cap // width
 
     def pick(peer, place):
-        index = sent_ref[pl.ds(peer * per + place, 1), :]
+        start = pl.multiple_of((peer * per + place) * width, width)
+        index = sent_ref[0, :, pl.ds(start, width)]
         return gather_strip(index, spread_ref, 0, source_strips // 2, lambda strip: strip)
 
     def send(step, carry):
@@ -166,7 +167,7 @@
 
         def step(j, carry):
             found = gather_strip(
-                list_ref[pl.ds(j, 1), :],
+                list_ref[0, pl.ds(j, 1), :],
                 spread_recv_ref,
                 phase * pairs_half,
                 pairs_half,
@@ -176,7 +177,7 @@
             out_ref[:, where] = found if phase == 0 else out_ref[:, where] + found
             return carry
 
-        lax.fori_loop(0, list_ref.shape[0], step, 0, unroll=2)
+        lax.fori_loop(0, list_ref.shape[1], step, 0, unroll=4)
     wait_sends(columns, me, send_ref, recv_ref, send_sems, recv_sems)
 
 
@@ -223,10 +224,14 @@
     )
     change = flow - after * ratio
     weight_high, weight_low = split2(weight)
-    colour_grads = (
-        jnp.dot(grads_high, weight_high, preferred_element_type=F32)
-        + jnp.dot(grads_low, weight_high, preferred_element_type=F32)
-        + jnp.dot(grads_high, weight_low, preferred_element_type=F32)
+    both = jnp.dot(
+        jnp.concatenate([grads_high, grads_low], axis=0),
+        weight_high,
+        preferred_element_type=F32,
+    )
+    channels = grads.shape[0]
+    colour_grads = (both[:channels] + both[channels:]) + jnp.dot(
+        grads_high, weight_low, preferred_element_type=F32
     )
     sums = sum(jnp.dot(moments, piece, preferred_element_type=F32) for piece in split3(change))
     m00, m10, m01, m20, m02, m11 = (sums[i : i + 1] for i in range(6))
@@ -271,7 +276,7 @@
         centre_y = ((row_base + first + i) * 16 + 8).astype(F32)
         out_ref[:, i * depth : (i + 1) * depth] = one_tile(
             params_ref[:, i * depth : (i + 1) * depth],
-            grads_ref[i],
+            grads_ref[:, 0, i, :],
             length_ref[first + i],
             centre_x,
             centre_y,
@@ -281,12 +286,13 @@
         )
 
 
-GROUP = 16
+SLOT_GROUP = 16
+SPLAT_GROUP = 32
 ENTRY_BLOCK = 2048
 
 
-def scatter_group(group, blocks, spread_ref):
-    total = jnp.zeros((GROUP * 32, STRIP), F32)
+def scatter_group(group, size, blocks, spread_ref):
+    total = jnp.zeros((size * 32, STRIP), F32)
     column = lax.broadcasted_iota(jnp.int32, (STRIP, ENTRY_BLOCK), 0)
     for load_index, load_values in blocks:
         index = load_index()
@@ -294,14 +300,14 @@
         hot = jnp.where(column == (index & (STRIP - 1)), 1.0, 0.0).astype(BF16)
         high, low = split2(load_values())
         both = jnp.concatenate([high, low], axis=0)
-        for c in range(GROUP):
-            mask = jnp.where(strip == group * GROUP + c, 1.0, 0.0).astype(BF16)
+        for c in range(size):
+            mask = jnp.where(strip == group * size + c, 1.0, 0.0).astype(BF16)
             spread_ref[c * 32 : (c + 1) * 32, :] = both * mask
         total += lax.dot_general(
-            spread_ref[...], hot, (((1,), (1,)), ((), ())), preferred_element_type=F32
+            spread_ref[: size * 32, :], hot, (((1,), (1,)), ((), ())), preferred_element_type=F32
         )
     return [
-        total[c * 32 : c * 32 + 16] + total[c * 32 + 16 : c * 32 + 32] for c in range(GROUP)
+        total[c * 32 : c * 32 + 16] + total[c * 32 + 16 : c * 32 + 32] for c in range(size)
     ]
 
 
@@ -313,16 +319,23 @@
     barrier = greet(columns, me)
     half = columns // 2
     my_half = me // half
+    depth = list_ref.shape[2]
     entry_blocks = [
         (
-            lambda start=start: list_ref[:, start : start + ENTRY_BLOCK],
+            lambda start=start: jnp.concatenate(
+                [
+                    list_ref[0, row : row + 1, :]
+                    for row in range(start // depth, (start + ENTRY_BLOCK) // depth)
+                ],
+                axis=1,
+            ),
             lambda start=start: value_ref[:, start : start + ENTRY_BLOCK],
         )
-        for start in range(0, list_ref.shape[1], ENTRY_BLOCK)
+        for start in range(0, value_ref.shape[1], ENTRY_BLOCK)
     ]
     for phase in range(2):
         group = my_half if phase else 1 - my_half
-        strips = scatter_group(group, entry_blocks, spread_ref)
+        strips = scatter_group(group, SLOT_GROUP, entry_blocks, spread_ref)
         for c, rows in enumerate(strips):
             for part in range(STRIP // LANES):
                 start = c * STRIP + part * LANES
@@ -343,21 +356,21 @@
 
     per_block = ENTRY_BLOCK // cap
     for phase in range(2):
-        from_half = my_half if phase else 1 - my_half
+        from_half = 1 - my_half if phase else my_half
 
         def arrived(step, carry):
             source = from_half * half + lax.rem(me + step, half)
             copy_between(send_ref, recv_ref, send_sems, recv_sems, source, source).wait_recv()
             return carry
 
-        lax.fori_loop(phase, half, arrived, 0)
+        lax.fori_loop(1 - phase, half, arrived, 0)
         blocks = []
         for block in range(half // per_block):
             first = from_half * half + block * per_block
             blocks.append(
                 (
                     lambda first=first: sent_ref[
-                        :, pl.ds(pl.multiple_of(first * cap, LANES), ENTRY_BLOCK)
+                        0, :, pl.ds(pl.multiple_of(first * cap, LANES), ENTRY_BLOCK)
                     ],
                     lambda first=first: jnp.concatenate(
                         [recv_ref[first + i] for i in range(per_block)], axis=1
@@ -366,13 +379,13 @@
             )
 
         def splat_group(group, carry):
-            found = scatter_group(group, blocks, spread_ref)
+            found = scatter_group(group, SPLAT_GROUP, blocks, spread_ref)
             for c, rows in enumerate(found):
-                where = pl.ds(pl.multiple_of((group * GROUP + c) * STRIP, STRIP), STRIP)
+                where = pl.ds(pl.multiple_of((group * SPLAT_GROUP + c) * STRIP, STRIP), STRIP)
                 out_ref[:, where] = rows if phase == 0 else out_ref[:, where] + rows
             return carry
 
-        lax.fori_loop(0, out_ref.shape[1] // (GROUP * STRIP), splat_group, 0)
+        lax.fori_loop(0, out_ref.shape[1] // (SPLAT_GROUP * STRIP), splat_group, 0)
     wait_sends(columns, me, send_ref, recv_ref, send_sems, recv_sems)
 
 
@@ -405,13 +418,12 @@
         ),
         name="receive_entries",
     )(
-        send_slots.reshape(slot_count // width, width),
+        send_slots,
         splats,
-        tile_lists.reshape(entry_count // STRIP, STRIP),
-    )
-    per_step = 2
+        tile_lists,
+    )
+    per_step = math.gcd(tile_count, 8)
     channels, pixels = pixel_grads.shape[0], pixel_grads.shape[3]
-    grads_here = jnp.moveaxis(pixel_grads[:, 0], 1, 0)
     entry_grads = pl.pallas_call(
         functools.partial(tile_kernel, per_step),
         out_shape=jax.ShapeDtypeStruct((features, entry_count), F32),
@@ -419,26 +431,26 @@
         in_specs=[
             pl.BlockSpec(memory_space=pltpu.SMEM),
             pl.BlockSpec((features, per_step * depth), lambda i: (0, i)),
-            pl.BlockSpec((per_step, channels, pixels), lambda i: (i, 0, 0)),
+            pl.BlockSpec((channels, 1, per_step, pixels), lambda i: (0, 0, i, 0)),
         ],
         out_specs=pl.BlockSpec((features, per_step * depth), lambda i: (0, i)),
         compiler_params=params_of(),
         name="tile_grads",
-    )(tile_lengths.reshape(tile_count), all_params, grads_here)
+    )(tile_lengths.reshape(tile_count), all_params, pixel_grads)
     partial_grads = pl.pallas_call(
         return_kernel,
         out_shape=jax.ShapeDtypeStruct((features, local_count), F32),
         in_specs=[whole(), whole(), whole()],
         out_specs=whole(),
-        scratch_shapes=[pltpu.VMEM((GROUP * 32, ENTRY_BLOCK), BF16)] + exchange,
+        scratch_shapes=[pltpu.VMEM((SPLAT_GROUP * 32, ENTRY_BLOCK), BF16)] + exchange,
         compiler_params=pltpu.CompilerParams(
             vmem_limit_bytes=VMEM_BYTES, collective_id=1, has_side_effects=True
         ),
         name="return_grads",
     )(
-        tile_lists.reshape(1, entry_count),
+        tile_lists,
         entry_grads,
-        send_slots.reshape(1, slot_count),
+        send_slots,
     )
     other = lax.ppermute(partial_grads, "narrow", [(0, 1), (1, 0)])
     return partial_grads + other

time: 93.9 us -> 83.6 us (0.89)
  Pallas kernels: 84.3 us -> 75.9 us
  other arithmetic: 2.55 us -> 1.08 us
    pallas_call x1, Pallas kernels: 22 us -> 18 us  [body(): pl.pallas_call(functools.partial(tile_kernel, per_step), out_shape=jax.Sh...]
    pallas_call x1, Pallas kernels: 30.6 us -> 27.5 us  [body(): pl.pallas_call(receive_kernel, out_shape=jax.ShapeDtypeStruct((features,...]
    unnamed x1 -> x0, other arithmetic: 1.48 us -> none
    pallas_call x1, Pallas kernels: 31.8 us -> 30.4 us  [body(): pl.pallas_call(return_kernel, out_shape=jax.ShapeDtypeStruct((features, l...]
    unnamed x11 -> x12, local copies, waits for them, and re-layouts: 3.89 us -> 3.39 us
where the time goes in v3:
time: 83.6 us; the launch traced here: 83.2 us
  Pallas kernels  75.9 us (91%)
  local copies, waits for them, and re-layouts  3.39 us (4%)
  waiting for transfers between devices  2.65 us (3%)
  other arithmetic  1.08 us (1%)
    pallas_call x1, Pallas kernels, body(): pl.pallas_call(return_kernel, out_shape=jax.ShapeDtypeStruct((features, l...  30.4 us
    pallas_call x1, Pallas kernels, body(): pl.pallas_call(receive_kernel, out_shape=jax.ShapeDtypeStruct((features,...  27.5 us
    pallas_call x1, Pallas kernels, body(): pl.pallas_call(functools.partial(tile_kernel, per_step), out_shape=jax.Sh...  18 us
    unnamed x12, local copies, waits for them, and re-layouts  3.39 us
    ppermute x1, waiting for transfers between devices, body(): other = lax.ppermute(partial_grads, 'narrow', [(0, 1), (1, 0)])  2.65 us
  transfers between devices with their start and end apart: 1, of which 1 were waited for; matrix products, arithmetic and copies ran while one was open for 0% of the time, Pallas kernels for 0%

profile of v3, /device:TPU:0, one launch (start us, length us, event | category | flops | bytes accessed | tf_op | source)
XLA Modules:
  0.0 83.2 jit_solution(8243193620597039351)
XLA Ops:
  0.0 0.0 copy-start
  0.0 1.2 %copy-done = f32[16,16384]{1,0:T(8,128)S(1)} copy-done((f32[16,16384]{1,0:T(8,128)S(1)}, f32[16,16384]{1,0:T(8,128)}, u32[]{:S(2)}) %copy-start) | copy-done | bytes 1048600
  1.2 0.0 copy-start.2
  1.2 0.8 copy-done.2
  2.0 0.0 copy-start.4
  2.0 0.8 copy-done.4
  2.7 0.0 copy-start.1
  2.7 27.5 %receive_entries.1.params_ref = f32[16,8192]{1,0:T(8,128)S(1)} custom-call(s32[1,1,8192]{2,1,0:T(1,128)S(1)} %copy-done.4, f32[16,16384]{1,0:T(8,128)S(1)} %copy-done, s32[1,32,256]{2,1,0:T(8,128)S(1)} %copy-done.2), custom_call_target="tpu_custom_call" | custom-call | tf_op jit(solution)/shard_map/receive_entries/pallas_call | solution.py:406
  30.3 0.0 copy-start.5
  30.3 0.0 copy-done.1
  30.3 0.6 copy-done.5
  30.9 0.0 copy-start.3
  30.9 18.0 %tile_grads.1.value_ref = f32[16,8192]{1,0:T(8,128)S(1)} custom-call(s32[32]{0:T(128)S(1)} %bitcast.1, f32[16,8192]{1,0:T(8,128)S(1)} %receive_entries.1.params_ref, f32[10,1,32,256]{3,2,1,0:T(8,128)S(1)} %copy-done.1), custom_call_target="tpu_custom_call" | custom-call | tf_op jit(solution)/shard_map/tile_grads/pallas_call | solution.py:427
  48.9 0.0 copy-done.3
  48.9 30.4 %return_grads.1 = f32[16,16384]{1,0:T(8,128)S(1)} custom-call(s32[1,32,256]{2,1,0:T(8,128)S(1)} %copy-done.3, f32[16,8192]{1,0:T(8,128)S(1)} %tile_grads.1.value_ref, s32[1,1,8192]{2,1,0:T(1,128)S(1)} %copy-done.4), custom_call_target="tpu_custom_call" | custom-call | tf_op jit(solution)/shard_map/return_grads/pallas_call | solution.py:440
  79.3 0.1 collective-permute-start
  79.4 2.6 %collective-permute-done = f32[16,16384]{1,0:T(8,128)S(1)} collective-permute-done((f32[16,16384]{1,0:T(8,128)S(1)}, f32[16,16384]{1,0:T(8,128)S(1)}, u32[]{:S(2)}, u32[]{:S(2)}) %collective-permute-start) | collective-permute-done | bytes 1048608 | tf_op jit(solution)/shard_map/ppermute | solution.py:455
  82.1 1.1 %add.3 = f32[16,16384]{1,0:T(8,128)} add(f32[16,16384]{1,0:T(8,128)S(1)} %return_grads.1, f32[16,16384]{1,0:T(8,128)S(1)} %collective-permute-done) | non-fusion elementwise | flops 262144 | bytes 3145728 | tf_op jit(solution)/shard_map/add | solution.py:456
Async XLA Ops:
  0.0 1.2 %copy-start = (f32[16,16384]{1,0:T(8,128)S(1)}, f32[16,16384]{1,0:T(8,128)}, u32[]{:S(2)}) copy-start(f32[16,16384]{1,0:T(8,128)} %source_ref.1) | copy-start | bytes 3145732
  1.2 0.8 copy-start.2
  2.0 0.8 copy-start.4
  2.7 27.6 %copy-start.1 = (f32[10,1,32,256]{3,2,1,0:T(8,128)S(1)}, f32[10,1,32,256]{3,2,1,0:T(8,128)}, u32[]{:S(2)}) copy-start(f32[10,1,32,256]{3,2,1,0:T(8,128)} %grads_ref.1) | copy-start | bytes 983044
  30.3 0.7 copy-start.5
  30.9 18.0 %copy-start.3 = (s32[1,32,256]{2,1,0:T(8,128)S(1)}, s32[1,32,256]{2,1,0:T(8,128)}, u32[]{:S(2)}) copy-start(s32[1,32,256]{2,1,0:T(8,128)} %list_ref.3) | copy-start | bytes 98308
  79.3 2.7 %collective-permute-start = (f32[16,16384]{1,0:T(8,128)S(1)}, f32[16,16384]{1,0:T(8,128)S(1)}, u32[]{:S(2)}, u32[]{:S(2)}) collective-permute-start(f32[16,16384]{1,0:T(8,128)S(1)} %return_grads.1), channel_id=1, source_target_pairs={{0,1},{1,0},{2,3},{3,2},{4,5},{5,4},{6,7},{7,6},{8,9},{9,8},{10,11... | collective-permute-start | bytes 3145736 | tf_op jit(solution)/shard_map/ppermute | solution.py:455

commit v4 on v3

--- a/solution.py
+++ b/solution.py
@@ -286,7 +286,7 @@
         )
 
 
-SLOT_GROUP = 16
+SLOT_GROUP = 8
 SPLAT_GROUP = 32
 ENTRY_BLOCK = 2048
 
@@ -333,25 +333,28 @@
         )
         for start in range(0, value_ref.shape[1], ENTRY_BLOCK)
     ]
-    for phase in range(2):
-        group = my_half if phase else 1 - my_half
+    quarter = columns // 4
+    mine = me // quarter
+    beside = mine + 1 - 2 * lax.rem(mine, 2)
+    order = [lax.rem(mine + 2, 4), lax.rem(beside + 2, 4), beside, mine]
+    for part_at, group in enumerate(order):
         strips = scatter_group(group, SLOT_GROUP, entry_blocks, spread_ref)
         for c, rows in enumerate(strips):
             for part in range(STRIP // LANES):
                 start = c * STRIP + part * LANES
                 place = start % cap
-                send_ref[group * half + start // cap, :, place : place + LANES] = rows[
+                send_ref[group * quarter + start // cap, :, place : place + LANES] = rows[
                     :, part * LANES : (part + 1) * LANES
                 ]
-        if phase == 0:
+        if part_at == 0:
             pl.semaphore_wait(barrier, columns - 1)
 
         def send(step, carry):
-            peer = group * half + lax.rem(me + step, half)
+            peer = group * quarter + lax.rem(me + step, quarter)
             copy_between(send_ref, recv_ref, send_sems, recv_sems, peer, me).start()
             return carry
 
-        lax.fori_loop(phase, half, send, 0)
+        lax.fori_loop(part_at // 3, quarter, send, 0)
     recv_ref[me] = send_ref[me]
 
     per_block = ENTRY_BLOCK // cap

time: 83.6 us -> 83.1 us (level)
  no operation moved by 1% of the time
where the time goes in v4:
time: 83.1 us; the launch traced here: 82.9 us
  Pallas kernels  75.6 us (91%)
  local copies, waits for them, and re-layouts  3.39 us (4%)
  waiting for transfers between devices  2.65 us (3%)
  other arithmetic  1.08 us (1%)
    pallas_call x1, Pallas kernels, body(): pl.pallas_call(return_kernel, out_shape=jax.ShapeDtypeStruct((features, l...  30.1 us
    pallas_call x1, Pallas kernels, body(): pl.pallas_call(receive_kernel, out_shape=jax.ShapeDtypeStruct((features,...  27.5 us
    pallas_call x1, Pallas kernels, body(): pl.pallas_call(functools.partial(tile_kernel, per_step), out_shape=jax.Sh...  18 us
    unnamed x12, local copies, waits for them, and re-layouts  3.39 us
    ppermute x1, waiting for transfers between devices, body(): other = lax.ppermute(partial_grads, 'narrow', [(0, 1), (1, 0)])  2.65 us
  transfers between devices with their start and end apart: 1, of which 1 were waited for; matrix products, arithmetic and copies ran while one was open for 0% of the time, Pallas kernels for 0%

profile of v4, /device:TPU:0, one launch (start us, length us, event | category | flops | bytes accessed | tf_op | source)
XLA Modules:
  0.0 82.9 jit_solution(3346520666798857731)
XLA Ops:
  0.0 0.0 copy-start
  0.0 1.2 %copy-done = f32[16,16384]{1,0:T(8,128)S(1)} copy-done((f32[16,16384]{1,0:T(8,128)S(1)}, f32[16,16384]{1,0:T(8,128)}, u32[]{:S(2)}) %copy-start) | copy-done | bytes 1048600
  1.2 0.0 copy-start.2
  1.2 0.8 copy-done.2
  2.0 0.0 copy-start.4
  2.0 0.8 copy-done.4
  2.7 0.0 copy-start.1
  2.7 27.5 %receive_entries.1.params_ref = f32[16,8192]{1,0:T(8,128)S(1)} custom-call(s32[1,1,8192]{2,1,0:T(1,128)S(1)} %copy-done.4, f32[16,16384]{1,0:T(8,128)S(1)} %copy-done, s32[1,32,256]{2,1,0:T(8,128)S(1)} %copy-done.2), custom_call_target="tpu_custom_call" | custom-call | tf_op jit(solution)/shard_map/receive_entries/pallas_call | solution.py:409
  30.3 0.0 copy-start.5
  30.3 0.0 copy-done.1
  30.3 0.6 copy-done.5
  30.9 0.0 copy-start.3
  30.9 18.0 %tile_grads.1.value_ref = f32[16,8192]{1,0:T(8,128)S(1)} custom-call(s32[32]{0:T(128)S(1)} %bitcast.1, f32[16,8192]{1,0:T(8,128)S(1)} %receive_entries.1.params_ref, f32[10,1,32,256]{3,2,1,0:T(8,128)S(1)} %copy-done.1), custom_call_target="tpu_custom_call" | custom-call | tf_op jit(solution)/shard_map/tile_grads/pallas_call | solution.py:430
  48.9 0.0 copy-done.3
  48.9 30.1 %return_grads.1 = f32[16,16384]{1,0:T(8,128)S(1)} custom-call(s32[1,32,256]{2,1,0:T(8,128)S(1)} %copy-done.3, f32[16,8192]{1,0:T(8,128)S(1)} %tile_grads.1.value_ref, s32[1,1,8192]{2,1,0:T(1,128)S(1)} %copy-done.4), custom_call_target="tpu_custom_call" | custom-call | tf_op jit(solution)/shard_map/return_grads/pallas_call | solution.py:443
  79.1 0.1 collective-permute-start
  79.1 2.6 %collective-permute-done = f32[16,16384]{1,0:T(8,128)S(1)} collective-permute-done((f32[16,16384]{1,0:T(8,128)S(1)}, f32[16,16384]{1,0:T(8,128)S(1)}, u32[]{:S(2)}, u32[]{:S(2)}) %collective-permute-start) | collective-permute-done | bytes 1048608 | tf_op jit(solution)/shard_map/ppermute | solution.py:458
  81.8 1.1 %add.3 = f32[16,16384]{1,0:T(8,128)} add(f32[16,16384]{1,0:T(8,128)S(1)} %return_grads.1, f32[16,16384]{1,0:T(8,128)S(1)} %collective-permute-done) | non-fusion elementwise | flops 262144 | bytes 3145728 | tf_op jit(solution)/shard_map/add | solution.py:459
Async XLA Ops:
  0.0 1.2 %copy-start = (f32[16,16384]{1,0:T(8,128)S(1)}, f32[16,16384]{1,0:T(8,128)}, u32[]{:S(2)}) copy-start(f32[16,16384]{1,0:T(8,128)} %source_ref.1) | copy-start | bytes 3145732
  1.2 0.8 copy-start.2
  2.0 0.8 copy-start.4
  2.7 27.6 %copy-start.1 = (f32[10,1,32,256]{3,2,1,0:T(8,128)S(1)}, f32[10,1,32,256]{3,2,1,0:T(8,128)}, u32[]{:S(2)}) copy-start(f32[10,1,32,256]{3,2,1,0:T(8,128)} %grads_ref.1) | copy-start | bytes 983044
  30.3 0.7 copy-start.5
  30.9 18.0 %copy-start.3 = (s32[1,32,256]{2,1,0:T(8,128)S(1)}, s32[1,32,256]{2,1,0:T(8,128)}, u32[]{:S(2)}) copy-start(s32[1,32,256]{2,1,0:T(8,128)} %list_ref.3) | copy-start | bytes 98308
  79.1 2.7 %collective-permute-start = (f32[16,16384]{1,0:T(8,128)S(1)}, f32[16,16384]{1,0:T(8,128)S(1)}, u32[]{:S(2)}, u32[]{:S(2)}) collective-permute-start(f32[16,16384]{1,0:T(8,128)S(1)} %return_grads.1), channel_id=1, source_target_pairs={{0,1},{1,0},{2,3},{3,2},{4,5},{5,4},{6,7},{7,6},{8,9},{9,8},{10,11... | collective-permute-start | bytes 3145736 | tf_op jit(solution)/shard_map/ppermute | solution.py:458
